TPU v7x, 32 devices: a whole 2x2x4 slice. The times are simulated.
32 devices in a mesh: seq: 8 (over z, x), head: 4 (over y, core).
Axes of the slice: x: 2, y: 2, z: 4, core: 2. Of those that a mesh axis runs over, the one named last changes fastest.
Arguments:
- inputs: float32 [8192, 4096], P('seq', 'head'), may hold values from -6 to 6
- cotangent: float32 [8192, 4096], P('seq', 'head'), may hold values from -1.5 to 1.5
- b_proj: float32 [8192, 128], P('seq'), may hold values from -1.8 to 1.8
- c_proj: float32 [8192, 128], P('seq'), may hold values from -1.8 to 1.8
- decay_rate: float32 [64], P('head'), may hold values from 1e-06 to 0.0001
- level_weight: float32 [8, 64, 8192], P(None, 'head', 'seq'), may hold values from 0 to 2, as said below
- starts: int32 [128], P('seq'), may hold values from 0 to 1, as said below
Outputs:
- grad_x: float32 [8192, 4096], P('seq', 'head')
- grad_b: float32 [8192, 128], P(('seq', 'head'))
- grad_c: float32 [8192, 128], P(('seq', 'head'))
- grad_level: float32 [8, 64, 8192], P(None, 'head', 'seq')
Inputs may be any that keep to these rules, and one draw needn't show every extreme that they name: `starts`: exactly two of the 128 stretches carry 1. `level_weight`: positive.
All inputs are finite; a program needn't handle non-finite values.
Results may differ from a plain program's by a relative error of at most 0.0001.
Values sent between devices are 32-bit elements; how exact they have to be, the bound alone decides.
No kernel may reach another device: no remote copies, remote signals or barrier semaphores. Data moves between devices by JAX's collectives and lax.ppermute only.
A program may use at most 128 MiB of HBM per device.

v0:
```python
import jax
import jax.numpy as jnp
from jax import lax
from jax.sharding import PartitionSpec as P

STRETCH = 64


def from_partner(x, axis, apart):
    return lax.ppermute(x, axis, [(i, i ^ 1 << apart) for i in range(lax.axis_size(axis))])


def local(inputs, cotangent, b_proj, c_proj, decay_rate, level_weight, starts):
    highest = lax.Precision.HIGHEST
    rows_dev = inputs.shape[0]
    head_count = decay_rate.shape[0]
    width = inputs.shape[1] // head_count
    seq_count = lax.axis_size("seq")
    seq_bits = seq_count.bit_length() - 1
    stretch_count = rows_dev // STRETCH
    stretch_bits = stretch_count.bit_length() - 1
    seq_index = lax.axis_index("seq")
    level_count = level_weight.shape[0]
    level_scale = (STRETCH * 2.0 ** jnp.arange(level_count, dtype=jnp.float32)) ** (-0.5)
    level_vals = level_weight * level_scale[:, None, None]
    position = (seq_index * rows_dev + jnp.arange(rows_dev) - seq_count * rows_dev // 2).astype(
        jnp.float32
    )
    decay_query = jnp.exp(-decay_rate[:, None] * position[None, :])
    decay_key = jnp.exp(decay_rate[:, None] * position[None, :])
    open_flag = 1.0 - starts.astype(jnp.float32)
    prefix_open = jnp.cumprod(open_flag)
    suffix_open = jnp.concatenate(
        [jnp.cumprod(open_flag[::-1])[::-1][1:], jnp.ones((1,), jnp.float32)]
    )
    device_clean = prefix_open[stretch_count - 1]
    prefix_rows = jnp.repeat(prefix_open, STRETCH)
    suffix_rows = jnp.repeat(suffix_open, STRETCH)
    x_heads = inputs.reshape(rows_dev, head_count, width)
    cot_heads = cotangent.reshape(rows_dev, head_count, width)
    key_weight = decay_key * suffix_rows[None, :]
    tail_total = jnp.einsum(
        "sn,shp->hnp", b_proj, x_heads * key_weight.T[:, :, None], precision=highest
    )
    query_weight = decay_query * prefix_rows[None, :]
    cross_level = level_vals[stretch_bits + 1 :]
    head_totals = jnp.einsum(
        "tn,kthp->khnp",
        c_proj,
        cot_heads[None] * jnp.transpose(cross_level * query_weight[None], (0, 2, 1))[..., None],
        precision=highest,
    )
    own_clean = device_clean
    before_clean = jnp.float32(1.0)
    after_clean = jnp.float32(1.0)
    carried = head_totals
    fwd_gates = []
    rev_totals = []
    rev_gates = []
    upper_list = []
    for level_bit in range(seq_bits):
        upper_half = (seq_index // 2**level_bit % 2).astype(jnp.float32)
        upper_list.append(upper_half)
        payload = (carried, own_clean)
        received = from_partner((payload[0], payload[1]), "seq", level_bit)
        far_heads = received[0]
        far_clean = received[len(received) - 1]
        rev_totals.append((1.0 - upper_half) * far_heads[0])
        rev_gates.append((1.0 - upper_half) * after_clean)
        fwd_gates.append(upper_half * before_clean)
        carried = upper_half * (far_heads[1:] + far_clean * carried[1:]) + (1.0 - upper_half) * (
            carried[1:] + own_clean * far_heads[1:]
        )
        before_clean = upper_half * far_clean * before_clean + (1.0 - upper_half) * before_clean
        after_clean = (1.0 - upper_half) * far_clean * after_clean + upper_half * after_clean
        own_clean = own_clean * far_clean
    all_tail, all_clean = (
        lax.all_gather(tail_total[None], "seq", axis=0, tiled=True),
        lax.all_gather(device_clean[None], "seq", axis=0, tiled=True),
    )
    zero_count = jnp.cumsum(1.0 - all_clean)
    device_ids = jnp.arange(seq_count)
    weight_rows = []
    for level_bit in range(seq_bits):
        stride = 2**level_bit
        block_base = (seq_index // stride ^ 1) * stride
        block_end = block_base + stride - 1
        end_count = jnp.sum(jnp.where(device_ids == block_end, zero_count, 0.0))
        inside = (
            (device_ids >= block_base) & (device_ids <= block_end) & (end_count - zero_count == 0.0)
        )
        weight_rows.append(jnp.where(inside, 1.0, 0.0) * upper_list[level_bit])
    fwd_state = jnp.einsum("km,mhnp->khnp", jnp.stack(weight_rows), all_tail, precision=highest)
    rev_state = jnp.stack(rev_totals)
    fwd_gate = jnp.stack(fwd_gates)
    rev_gate = jnp.stack(rev_gates)
    query_gate = fwd_gate[:, None, None] * query_weight[None]
    lam_query = cross_level * query_gate
    weighted_cot = cot_heads[None] * jnp.transpose(lam_query, (0, 2, 1))[..., None]
    grad_c_cross = jnp.einsum("kthp,khnp->tn", weighted_cot, fwd_state, precision=highest)
    projected = jnp.einsum("tn,khnp->kthp", c_proj, fwd_state, precision=highest)
    grad_lam_cross = query_gate * jnp.transpose(
        jnp.sum(projected * cot_heads[None], axis=-1), (0, 2, 1)
    )
    rev_combined = jnp.einsum("k,khnp->hnp", rev_gate, rev_state, precision=highest)
    key_rows = key_weight.T[:, :, None]
    grad_x_cross = jnp.einsum("sn,hnp->shp", b_proj, rev_combined, precision=highest) * key_rows
    grad_b_cross = jnp.einsum("shp,hnp->sn", x_heads * key_rows, rev_combined, precision=highest)
    local_stretch = jnp.arange(rows_dev) // STRETCH
    differ = local_stretch[:, None] ^ local_stretch[None, :]
    local_level = jnp.zeros_like(differ)
    for level_bit in range(stretch_bits):
        local_level = local_level + (differ >= 2**level_bit).astype(jnp.int32)
    local_doc = jnp.cumsum(starts)[local_stretch]
    row_ids = jnp.arange(rows_dev)
    valid = (row_ids[:, None] >= row_ids[None, :]) & (local_doc[:, None] == local_doc[None, :])
    scores = jnp.dot(c_proj, b_proj.T, precision=highest)

    def head_step(mixed_sum, pieces):
        x_one, cot_one, query_decay, key_decay, lam_one = pieces
        decayed = jnp.where(valid, query_decay[:, None] * key_decay[None, :], 0.0)
        lam_pair = jnp.zeros((rows_dev, rows_dev), jnp.float32)
        for level in range(stretch_bits + 1):
            lam_pair = jnp.where(local_level == level, lam_one[level][:, None], lam_pair)
        inner = jnp.dot(cot_one, x_one.T, precision=highest)
        kernel = decayed * lam_pair
        weighted = kernel * scores
        plain = decayed * scores * inner
        grad_x_one = jnp.dot(weighted.T, cot_one, precision=highest)
        grad_lam_one = jnp.stack(
            [
                jnp.sum(jnp.where(local_level == level, plain, 0.0), axis=1)
                for level in range(stretch_bits + 1)
            ]
        )
        return (mixed_sum + kernel * inner, (grad_x_one, grad_lam_one))

    pieces = (
        jnp.transpose(x_heads, (1, 0, 2)),
        jnp.transpose(cot_heads, (1, 0, 2)),
        decay_query,
        decay_key,
        jnp.transpose(level_vals[: stretch_bits + 1], (1, 0, 2)),
    )
    mixed_total, (grad_x_local, grad_lam_local) = lax.scan(
        head_step, jnp.zeros((rows_dev, rows_dev), jnp.float32), pieces
    )
    local_c = grad_c_cross + jnp.dot(mixed_total, b_proj, precision=highest)
    local_b = grad_b_cross + jnp.dot(mixed_total.T, c_proj, precision=highest)
    grad_x = (jnp.transpose(grad_x_local, (1, 0, 2)) + grad_x_cross).reshape(
        rows_dev, head_count * width
    )
    grad_level = (
        jnp.concatenate([jnp.transpose(grad_lam_local, (1, 0, 2)), grad_lam_cross], 0)
        * level_scale[:, None, None]
    )
    grad_b, grad_c = (
        lax.psum_scatter(local_b, "head", scatter_dimension=0, tiled=True),
        lax.psum_scatter(local_c, "head", scatter_dimension=0, tiled=True),
    )
    return (grad_x, grad_b, grad_c, grad_level)


def solution(mesh):
    return jax.shard_map(
        local,
        mesh=mesh,
        in_specs=(
            P("seq", "head"),
            P("seq", "head"),
            P("seq", None),
            P("seq", None),
            P("head"),
            P(None, "head", "seq"),
            P("seq"),
        ),
        out_specs=(
            P("seq", "head"),
            P(("seq", "head"), None),
            P(("seq", "head"), None),
            P(None, "head", "seq"),
        ),
        check_vma=False,
    )
```

profile of v0, /device:TPU:0, one launch (start us, length us, event | category | flops | bytes accessed | tf_op | source)
XLA Modules:
  0.0 729.3 jit_solution(16242255150893106869)
XLA Ops:
  25.5 21.2 %all-reduce = f32[8]{0:T(128)S(1)} all-reduce(f32[8]{0:T(128)S(1)} %bitcast_dynamic-update-slice_fusion), channel_id=2, replica_groups=mesh['seq'=8,'head'=4] {'seq'}, use_global_device_ids=true, to_apply=%add | all-reduce | flops 8 | bytes 64
  62.4 33.9 %all-gather.4.cloned.1.call-done = f32[128,128,64]{1,2,0:T(8,128)} async-done(((f32[16,128,64]{1,2,0:T(8,128)}), f32[128,128,64]{1,2,0:T(8,128)}) %all-gather.4.cloned.1.call-update) | async-done | bytes 4194320 | tf_op jit(solution)/shard_map/all_gather | solution.py:78
  104.6 11.6 %fusion.30 = f32[3,1024,16]{1,2,0:T(8,128)S(1)} fusion(f32[1024,16,64]{0,2,1:T(8,128)S(1)} %bitcast.202, f32[3,16,128,64]{2,0,3,1:T(4,128)S(1)} %fusion.38, f32[1024,128]{1,0:T(8,128)S(1)} %copy-done.5), kind=kOutput, calls=%fused_computation.50 | convolution fusion | flops 4838080512 | bytes 6488064 | tf_op jit(solution)/shard_map/tn,khnp->kthp/dot_general | solution.py:101
  118.0 11.2 %fusion.50 = f32[3,16,128,64]{2,3,1,0:T(8,128)} fusion(f32[3,1024,16]{1,2,0:T(8,128)S(1)} %get-tuple-element.287, f32[1024,16,64]{0,2,1:T(8,128)S(1)} %bitcast.203, f32[1024,128]{1,0:T(8,128)S(1)} %copy-done.5), kind=kOutput, calls=%fused_computation.73 | convolution fusion | flops 4834983936 | bytes 6488064 | tf_op jit(solution)/shard_map/tn,kthp->khnp/dot_general | solution.py:47
  147.3 17.1 %collective-permute-done.2 = f32[3,16,128,64]{2,3,1,0:T(8,128)} collective-permute-done((f32[3,16,128,64]{2,3,1,0:T(8,128)}, f32[3,16,128,64]{2,3,1,0:T(8,128)}, u32[]{:S(2)}, u32[]{:S(2)}) %collective-permute-start.2) | collective-permute-done | bytes 1572896 | tf_op jit(solution)/shard_map/ppermute | solution.py:10
  169.6 465.9 %while.16 = (s32[]{:T(128)}, f32[1024,1024]{0,1:T(8,128)}, f32[16,1024,64]{1,2,0:T(8,128)}, f32[16,5,1024]{2,0,1:T(8,128)}, f32[16,1024]{1,0:T(8,128)}, /*index=...) while((s32[]{:T(128)}, f32[1024,1024]{0,1:T(8,128)}, ...), condition=%wide.region_7.8_spmd.clone.clone, body=%wide.region_1.0_spmd.clone.clone.sunk | while | flops 1703930880 | bytes 43289372 | solution.py:145
  171.4 11.7 %multiply_multiply_fusion.4 = (f32[1024,1024]{0,1:T(8,128)S(1)}, f32[1024,1024]{0,1:T(8,128)}) fusion(f32[1024,1024]{0,1:T(8,128)} %get-tuple-element.459, s32[1024]{0:T(1024)S(1)} %get-tuple-element.460, f32[1024]{0:T(1024)S(1)} %bitcast.219, f32[1024]{0:T(1024)S(1)} %bitcast.221, f32[1024]{0:T(1024)S(1)} %bitcast.231, f32[1024]{0:T(1024)S(1)} %bitcast.225, ...), kind=kOutput, calls=%fused_computation.14.clone.1 | convolution fusion | flops 839909376 | bytes 17348096 | tf_op jit(solution)/shard_map/while/body/eval_jaxpr/dot_general | solution.py:125
  200.1 12.1 %multiply_multiply_fusion.4 = (f32[1024,1024]{0,1:T(8,128)S(1)}, f32[1024,1024]{0,1:T(8,128)}) fusion(f32[1024,1024]{0,1:T(8,128)} %get-tuple-element.459, s32[1024]{0:T(1024)S(1)} %get-tuple-element.460, f32[1024]{0:T(1024)S(1)} %bitcast.219, f32[1024]{0:T(1024)S(1)} %bitcast.221, f32[1024]{0:T(1024)S(1)} %bitcast.231, f32[1024]{0:T(1024)S(1)} %bitcast.225, ...), kind=kOutput, calls=%fused_computation.14.clone.1 | convolution fusion | flops 839909376 | bytes 17348096 | tf_op jit(solution)/shard_map/while/body/eval_jaxpr/dot_general | solution.py:125
  229.2 12.1 %multiply_multiply_fusion.4 = (f32[1024,1024]{0,1:T(8,128)S(1)}, f32[1024,1024]{0,1:T(8,128)}) fusion(f32[1024,1024]{0,1:T(8,128)} %get-tuple-element.459, s32[1024]{0:T(1024)S(1)} %get-tuple-element.460, f32[1024]{0:T(1024)S(1)} %bitcast.219, f32[1024]{0:T(1024)S(1)} %bitcast.221, f32[1024]{0:T(1024)S(1)} %bitcast.231, f32[1024]{0:T(1024)S(1)} %bitcast.225, ...), kind=kOutput, calls=%fused_computation.14.clone.1 | convolution fusion | flops 839909376 | bytes 17348096 | tf_op jit(solution)/shard_map/while/body/eval_jaxpr/dot_general | solution.py:125
  241.4 9.5 %fusion.106 = f32[16,1024,64]{1,2,0:T(8,128)} fusion(f32[16,1024,64]{1,2,0:T(8,128)} %get-tuple-element.434, s32[]{:T(128)S(6)} %copy.113, f32[1024,1024]{0,1:T(8,128)S(1)} %copy-done.6, f32[1024]{0:T(1024)S(1)} %bitcast.232, f32[1024]{0:T(1024)S(1)} %bitcast.226, f32[1024]{0:T(1024)S(1)} %bitcast.228, f32[1024]{0:T(1024)S(1)} %bitcast.230, ...), kind=kOutput, calls=%fused_computation.26.clone.1 | convolution fusion | flops 835715072 | bytes 4764672 | tf_op jit(solution)/shard_map/while/body/eval_jaxpr/dot_general | solution.py:129
  258.3 12.1 %multiply_multiply_fusion.4 = (f32[1024,1024]{0,1:T(8,128)S(1)}, f32[1024,1024]{0,1:T(8,128)}) fusion(f32[1024,1024]{0,1:T(8,128)} %get-tuple-element.459, s32[1024]{0:T(1024)S(1)} %get-tuple-element.460, f32[1024]{0:T(1024)S(1)} %bitcast.219, f32[1024]{0:T(1024)S(1)} %bitcast.221, f32[1024]{0:T(1024)S(1)} %bitcast.231, f32[1024]{0:T(1024)S(1)} %bitcast.225, ...), kind=kOutput, calls=%fused_computation.14.clone.1 | convolution fusion | flops 839909376 | bytes 17348096 | tf_op jit(solution)/shard_map/while/body/eval_jaxpr/dot_general | solution.py:125
  270.5 9.5 %fusion.106 = f32[16,1024,64]{1,2,0:T(8,128)} fusion(f32[16,1024,64]{1,2,0:T(8,128)} %get-tuple-element.434, s32[]{:T(128)S(6)} %copy.113, f32[1024,1024]{0,1:T(8,128)S(1)} %copy-done.6, f32[1024]{0:T(1024)S(1)} %bitcast.232, f32[1024]{0:T(1024)S(1)} %bitcast.226, f32[1024]{0:T(1024)S(1)} %bitcast.228, f32[1024]{0:T(1024)S(1)} %bitcast.230, ...), kind=kOutput, calls=%fused_computation.26.clone.1 | convolution fusion | flops 835715072 | bytes 4764672 | tf_op jit(solution)/shard_map/while/body/eval_jaxpr/dot_general | solution.py:129
  287.5 12.1 %multiply_multiply_fusion.4 = (f32[1024,1024]{0,1:T(8,128)S(1)}, f32[1024,1024]{0,1:T(8,128)}) fusion(f32[1024,1024]{0,1:T(8,128)} %get-tuple-element.459, s32[1024]{0:T(1024)S(1)} %get-tuple-element.460, f32[1024]{0:T(1024)S(1)} %bitcast.219, f32[1024]{0:T(1024)S(1)} %bitcast.221, f32[1024]{0:T(1024)S(1)} %bitcast.231, f32[1024]{0:T(1024)S(1)} %bitcast.225, ...), kind=kOutput, calls=%fused_computation.14.clone.1 | convolution fusion | flops 839909376 | bytes 17348096 | tf_op jit(solution)/shard_map/while/body/eval_jaxpr/dot_general | solution.py:125
  316.6 12.1 %multiply_multiply_fusion.4 = (f32[1024,1024]{0,1:T(8,128)S(1)}, f32[1024,1024]{0,1:T(8,128)}) fusion(f32[1024,1024]{0,1:T(8,128)} %get-tuple-element.459, s32[1024]{0:T(1024)S(1)} %get-tuple-element.460, f32[1024]{0:T(1024)S(1)} %bitcast.219, f32[1024]{0:T(1024)S(1)} %bitcast.221, f32[1024]{0:T(1024)S(1)} %bitcast.231, f32[1024]{0:T(1024)S(1)} %bitcast.225, ...), kind=kOutput, calls=%fused_computation.14.clone.1 | convolution fusion | flops 839909376 | bytes 17348096 | tf_op jit(solution)/shard_map/while/body/eval_jaxpr/dot_general | solution.py:125
  328.7 9.5 %fusion.106 = f32[16,1024,64]{1,2,0:T(8,128)} fusion(f32[16,1024,64]{1,2,0:T(8,128)} %get-tuple-element.434, s32[]{:T(128)S(6)} %copy.113, f32[1024,1024]{0,1:T(8,128)S(1)} %copy-done.6, f32[1024]{0:T(1024)S(1)} %bitcast.232, f32[1024]{0:T(1024)S(1)} %bitcast.226, f32[1024]{0:T(1024)S(1)} %bitcast.228, f32[1024]{0:T(1024)S(1)} %bitcast.230, ...), kind=kOutput, calls=%fused_computation.26.clone.1 | convolution fusion | flops 835715072 | bytes 4764672 | tf_op jit(solution)/shard_map/while/body/eval_jaxpr/dot_general | solution.py:129
  345.7 12.1 %multiply_multiply_fusion.4 = (f32[1024,1024]{0,1:T(8,128)S(1)}, f32[1024,1024]{0,1:T(8,128)}) fusion(f32[1024,1024]{0,1:T(8,128)} %get-tuple-element.459, s32[1024]{0:T(1024)S(1)} %get-tuple-element.460, f32[1024]{0:T(1024)S(1)} %bitcast.219, f32[1024]{0:T(1024)S(1)} %bitcast.221, f32[1024]{0:T(1024)S(1)} %bitcast.231, f32[1024]{0:T(1024)S(1)} %bitcast.225, ...), kind=kOutput, calls=%fused_computation.14.clone.1 | convolution fusion | flops 839909376 | bytes 17348096 | tf_op jit(solution)/shard_map/while/body/eval_jaxpr/dot_general | solution.py:125
  357.8 9.5 %fusion.106 = f32[16,1024,64]{1,2,0:T(8,128)} fusion(f32[16,1024,64]{1,2,0:T(8,128)} %get-tuple-element.434, s32[]{:T(128)S(6)} %copy.113, f32[1024,1024]{0,1:T(8,128)S(1)} %copy-done.6, f32[1024]{0:T(1024)S(1)} %bitcast.232, f32[1024]{0:T(1024)S(1)} %bitcast.226, f32[1024]{0:T(1024)S(1)} %bitcast.228, f32[1024]{0:T(1024)S(1)} %bitcast.230, ...), kind=kOutput, calls=%fused_computation.26.clone.1 | convolution fusion | flops 835715072 | bytes 4764672 | tf_op jit(solution)/shard_map/while/body/eval_jaxpr/dot_general | solution.py:129
  374.8 12.1 %multiply_multiply_fusion.4 = (f32[1024,1024]{0,1:T(8,128)S(1)}, f32[1024,1024]{0,1:T(8,128)}) fusion(f32[1024,1024]{0,1:T(8,128)} %get-tuple-element.459, s32[1024]{0:T(1024)S(1)} %get-tuple-element.460, f32[1024]{0:T(1024)S(1)} %bitcast.219, f32[1024]{0:T(1024)S(1)} %bitcast.221, f32[1024]{0:T(1024)S(1)} %bitcast.231, f32[1024]{0:T(1024)S(1)} %bitcast.225, ...), kind=kOutput, calls=%fused_computation.14.clone.1 | convolution fusion | flops 839909376 | bytes 17348096 | tf_op jit(solution)/shard_map/while/body/eval_jaxpr/dot_general | solution.py:125
  403.9 12.1 %multiply_multiply_fusion.4 = (f32[1024,1024]{0,1:T(8,128)S(1)}, f32[1024,1024]{0,1:T(8,128)}) fusion(f32[1024,1024]{0,1:T(8,128)} %get-tuple-element.459, s32[1024]{0:T(1024)S(1)} %get-tuple-element.460, f32[1024]{0:T(1024)S(1)} %bitcast.219, f32[1024]{0:T(1024)S(1)} %bitcast.221, f32[1024]{0:T(1024)S(1)} %bitcast.231, f32[1024]{0:T(1024)S(1)} %bitcast.225, ...), kind=kOutput, calls=%fused_computation.14.clone.1 | convolution fusion | flops 839909376 | bytes 17348096 | tf_op jit(solution)/shard_map/while/body/eval_jaxpr/dot_general | solution.py:125
  416.1 9.5 %fusion.106 = f32[16,1024,64]{1,2,0:T(8,128)} fusion(f32[16,1024,64]{1,2,0:T(8,128)} %get-tuple-element.434, s32[]{:T(128)S(6)} %copy.113, f32[1024,1024]{0,1:T(8,128)S(1)} %copy-done.6, f32[1024]{0:T(1024)S(1)} %bitcast.232, f32[1024]{0:T(1024)S(1)} %bitcast.226, f32[1024]{0:T(1024)S(1)} %bitcast.228, f32[1024]{0:T(1024)S(1)} %bitcast.230, ...), kind=kOutput, calls=%fused_computation.26.clone.1 | convolution fusion | flops 835715072 | bytes 4764672 | tf_op jit(solution)/shard_map/while/body/eval_jaxpr/dot_general | solution.py:129
  433.0 12.1 %multiply_multiply_fusion.4 = (f32[1024,1024]{0,1:T(8,128)S(1)}, f32[1024,1024]{0,1:T(8,128)}) fusion(f32[1024,1024]{0,1:T(8,128)} %get-tuple-element.459, s32[1024]{0:T(1024)S(1)} %get-tuple-element.460, f32[1024]{0:T(1024)S(1)} %bitcast.219, f32[1024]{0:T(1024)S(1)} %bitcast.221, f32[1024]{0:T(1024)S(1)} %bitcast.231, f32[1024]{0:T(1024)S(1)} %bitcast.225, ...), kind=kOutput, calls=%fused_computation.14.clone.1 | convolution fusion | flops 839909376 | bytes 17348096 | tf_op jit(solution)/shard_map/while/body/eval_jaxpr/dot_general | solution.py:125
  445.2 9.5 %fusion.106 = f32[16,1024,64]{1,2,0:T(8,128)} fusion(f32[16,1024,64]{1,2,0:T(8,128)} %get-tuple-element.434, s32[]{:T(128)S(6)} %copy.113, f32[1024,1024]{0,1:T(8,128)S(1)} %copy-done.6, f32[1024]{0:T(1024)S(1)} %bitcast.232, f32[1024]{0:T(1024)S(1)} %bitcast.226, f32[1024]{0:T(1024)S(1)} %bitcast.228, f32[1024]{0:T(1024)S(1)} %bitcast.230, ...), kind=kOutput, calls=%fused_computation.26.clone.1 | convolution fusion | flops 835715072 | bytes 4764672 | tf_op jit(solution)/shard_map/while/body/eval_jaxpr/dot_general | solution.py:129
  462.1 12.1 %multiply_multiply_fusion.4 = (f32[1024,1024]{0,1:T(8,128)S(1)}, f32[1024,1024]{0,1:T(8,128)}) fusion(f32[1024,1024]{0,1:T(8,128)} %get-tuple-element.459, s32[1024]{0:T(1024)S(1)} %get-tuple-element.460, f32[1024]{0:T(1024)S(1)} %bitcast.219, f32[1024]{0:T(1024)S(1)} %bitcast.221, f32[1024]{0:T(1024)S(1)} %bitcast.231, f32[1024]{0:T(1024)S(1)} %bitcast.225, ...), kind=kOutput, calls=%fused_computation.14.clone.1 | convolution fusion | flops 839909376 | bytes 17348096 | tf_op jit(solution)/shard_map/while/body/eval_jaxpr/dot_general | solution.py:125
  474.3 9.5 %fusion.106 = f32[16,1024,64]{1,2,0:T(8,128)} fusion(f32[16,1024,64]{1,2,0:T(8,128)} %get-tuple-element.434, s32[]{:T(128)S(6)} %copy.113, f32[1024,1024]{0,1:T(8,128)S(1)} %copy-done.6, f32[1024]{0:T(1024)S(1)} %bitcast.232, f32[1024]{0:T(1024)S(1)} %bitcast.226, f32[1024]{0:T(1024)S(1)} %bitcast.228, f32[1024]{0:T(1024)S(1)} %bitcast.230, ...), kind=kOutput, calls=%fused_computation.26.clone.1 | convolution fusion | flops 835715072 | bytes 4764672 | tf_op jit(solution)/shard_map/while/body/eval_jaxpr/dot_general | solution.py:129
  491.2 12.1 %multiply_multiply_fusion.4 = (f32[1024,1024]{0,1:T(8,128)S(1)}, f32[1024,1024]{0,1:T(8,128)}) fusion(f32[1024,1024]{0,1:T(8,128)} %get-tuple-element.459, s32[1024]{0:T(1024)S(1)} %get-tuple-element.460, f32[1024]{0:T(1024)S(1)} %bitcast.219, f32[1024]{0:T(1024)S(1)} %bitcast.221, f32[1024]{0:T(1024)S(1)} %bitcast.231, f32[1024]{0:T(1024)S(1)} %bitcast.225, ...), kind=kOutput, calls=%fused_computation.14.clone.1 | convolution fusion | flops 839909376 | bytes 17348096 | tf_op jit(solution)/shard_map/while/body/eval_jaxpr/dot_general | solution.py:125
  520.3 12.1 %multiply_multiply_fusion.4 = (f32[1024,1024]{0,1:T(8,128)S(1)}, f32[1024,1024]{0,1:T(8,128)}) fusion(f32[1024,1024]{0,1:T(8,128)} %get-tuple-element.459, s32[1024]{0:T(1024)S(1)} %get-tuple-element.460, f32[1024]{0:T(1024)S(1)} %bitcast.219, f32[1024]{0:T(1024)S(1)} %bitcast.221, f32[1024]{0:T(1024)S(1)} %bitcast.231, f32[1024]{0:T(1024)S(1)} %bitcast.225, ...), kind=kOutput, calls=%fused_computation.14.clone.1 | convolution fusion | flops 839909376 | bytes 17348096 | tf_op jit(solution)/shard_map/while/body/eval_jaxpr/dot_general | solution.py:125
  549.4 12.1 %multiply_multiply_fusion.4 = (f32[1024,1024]{0,1:T(8,128)S(1)}, f32[1024,1024]{0,1:T(8,128)}) fusion(f32[1024,1024]{0,1:T(8,128)} %get-tuple-element.459, s32[1024]{0:T(1024)S(1)} %get-tuple-element.460, f32[1024]{0:T(1024)S(1)} %bitcast.219, f32[1024]{0:T(1024)S(1)} %bitcast.221, f32[1024]{0:T(1024)S(1)} %bitcast.231, f32[1024]{0:T(1024)S(1)} %bitcast.225, ...), kind=kOutput, calls=%fused_computation.14.clone.1 | convolution fusion | flops 839909376 | bytes 17348096 | tf_op jit(solution)/shard_map/while/body/eval_jaxpr/dot_general | solution.py:125
  578.5 12.1 %multiply_multiply_fusion.4 = (f32[1024,1024]{0,1:T(8,128)S(1)}, f32[1024,1024]{0,1:T(8,128)}) fusion(f32[1024,1024]{0,1:T(8,128)} %get-tuple-element.459, s32[1024]{0:T(1024)S(1)} %get-tuple-element.460, f32[1024]{0:T(1024)S(1)} %bitcast.219, f32[1024]{0:T(1024)S(1)} %bitcast.221, f32[1024]{0:T(1024)S(1)} %bitcast.231, f32[1024]{0:T(1024)S(1)} %bitcast.225, ...), kind=kOutput, calls=%fused_computation.14.clone.1 | convolution fusion | flops 839909376 | bytes 17348096 | tf_op jit(solution)/shard_map/while/body/eval_jaxpr/dot_general | solution.py:125
  607.6 12.1 %multiply_multiply_fusion.4 = (f32[1024,1024]{0,1:T(8,128)S(1)}, f32[1024,1024]{0,1:T(8,128)}) fusion(f32[1024,1024]{0,1:T(8,128)} %get-tuple-element.459, s32[1024]{0:T(1024)S(1)} %get-tuple-element.460, f32[1024]{0:T(1024)S(1)} %bitcast.219, f32[1024]{0:T(1024)S(1)} %bitcast.221, f32[1024]{0:T(1024)S(1)} %bitcast.231, f32[1024]{0:T(1024)S(1)} %bitcast.225, ...), kind=kOutput, calls=%fused_computation.14.clone.1 | convolution fusion | flops 839909376 | bytes 17348096 | tf_op jit(solution)/shard_map/while/body/eval_jaxpr/dot_general | solution.py:125
  619.7 9.5 %fusion.106 = f32[16,1024,64]{1,2,0:T(8,128)} fusion(f32[16,1024,64]{1,2,0:T(8,128)} %get-tuple-element.434, s32[]{:T(128)S(6)} %copy.113, f32[1024,1024]{0,1:T(8,128)S(1)} %copy-done.6, f32[1024]{0:T(1024)S(1)} %bitcast.232, f32[1024]{0:T(1024)S(1)} %bitcast.226, f32[1024]{0:T(1024)S(1)} %bitcast.228, f32[1024]{0:T(1024)S(1)} %bitcast.230, ...), kind=kOutput, calls=%fused_computation.26.clone.1 | convolution fusion | flops 835715072 | bytes 4764672 | tf_op jit(solution)/shard_map/while/body/eval_jaxpr/dot_general | solution.py:129
  636.8 22.2 %fusion.53 = f32[1024,128]{1,0:T(8,128)S(1)} fusion(f32[3,16,128,64]{2,0,3,1:T(4,128)S(1)} %fusion.38, f32[3,1024,16]{1,2,0:T(8,128)} %get-tuple-element.286, f32[1024,16,64]{0,2,1:T(8,128)} %bitcast.204), kind=kOutput, calls=%fused_computation.74 | convolution fusion | flops 4834983936 | bytes 6488064 | tf_op jit(solution)/shard_map/kthp,khnp->tn/dot_general | solution.py:100
  672.7 12.9 %collective-permute-done.4 = f32[1,16,128,64]{2,3,1,0:T(8,128)S(1)} collective-permute-done((f32[1,16,128,64]{2,3,1,0:T(8,128)S(1)}, f32[1,16,128,64]{2,3,1,0:T(8,128)S(1)}, u32[]{:S(2)}, u32[]{:S(2)}) %collective-permute-start.4) | collective-permute-done | bytes 524320 | tf_op jit(solution)/shard_map/ppermute | solution.py:10
  (241 shorter events, 310.2 us)
Async XLA Ops:
  7.2 6.3 copy-start
  7.2 89.2 %all-gather.4.cloned.1.call-start = ((), (), s32[]{:S(2)}) async-start(), calls=%async_computation.4 | async-start | bytes 4718592 | tf_op jit(solution)/shard_map/all_gather | solution.py:78
  12.7 7.9 %copy-start.11 = (u32[32]{0:T(128)S(1)}, u32[32]{0:T(128)}, u32[]{:S(2)}) copy-start(u32[32]{0:T(128)} %constant.177) | copy-start | bytes 388
  19.9 694.5 %reduce-scatter.5.cloned.1.call-start = ((), (), s32[]{:S(2)}) async-start(), calls=%async_computation.3 | async-start | bytes 655360 | tf_op jit(solution)/shard_map/reduce_scatter | solution.py:159
  22.5 34.3 %collective-permute-start = (f32[]{:T(128)}, f32[]{:T(128)}, u32[]{:S(2)}, u32[]{:S(2)}) collective-permute-start(f32[]{:T(128)} %bitcast.26), channel_id=1, source_target_pairs={{0,4},{4,0},{8,12},{12,8},{16,20},{20,16},{24,28},{28,24},{1,5},{5... | collective-permute-start | bytes 20 | tf_op jit(solution)/shard_map/ppermute | solution.py:10
  47.0 8.9 %copy-start.7 = (f32[8,16,1024]{2,1,0:T(8,128)S(1)}, f32[8,16,1024]{2,1,0:T(8,128)}, u32[]{:S(2)}) copy-start(f32[8,16,1024]{2,1,0:T(8,128)} %param.14) | copy-start | bytes 1572868
  52.4 52.2 %copy-start.5 = (f32[1024,128]{1,0:T(8,128)S(1)}, f32[1024,128]{1,0:T(8,128)}, u32[]{:S(2)}) copy-start(f32[1024,128]{1,0:T(8,128)} %param.12) | copy-start | bytes 1572868
  58.1 3.6 collective-permute-start.1
  96.3 8.3 %copy-start.1 = (f32[1024,1024]{0,1:T(8,128)S(1)}, f32[1024,1024]{0,1:T(8,128)}, u32[]{:S(2)}) copy-start(f32[1024,1024]{0,1:T(8,128)} %copy.54) | copy-start | bytes 12582916
  129.2 35.3 %collective-permute-start.2 = (f32[3,16,128,64]{2,3,1,0:T(8,128)}, f32[3,16,128,64]{2,3,1,0:T(8,128)}, u32[]{:S(2)}, u32[]{:S(2)}) collective-permute-start(f32[3,16,128,64]{2,3,1,0:T(8,128)} %fusion.50), channel_id=1, source_target_pairs={{0,4},{4,0},{8,12},{12,8},{16,20},{20,16},{24,28},{28,24},{1,5},{5... | collective-permute-start | bytes 4718600 | tf_op jit(solution)/shard_map/ppermute | solution.py:10
  168.6 490.4 %collective-permute-start.3 = (f32[2,16,128,64]{2,3,1,0:T(8,128)}, f32[2,16,128,64]{2,3,1,0:T(8,128)}, u32[]{:S(2)}, u32[]{:S(2)}) collective-permute-start(f32[2,16,128,64]{2,3,1,0:T(8,128)} %multiply_add_fusion), channel_id=1, source_target_pairs={{0,8},{4,12},{8,0},{12,4},{16,24},{20,28},{24,16},{28,20},{1,9},{5... | collective-permute-start | bytes 3145736 | tf_op jit(solution)/shard_map/ppermute | solution.py:10
  171.4 11.7 %copy-start.6 = (f32[1024,1024]{0,1:T(8,128)S(1)}, f32[1024,1024]{0,1:T(8,128)}, u32[]{:S(2)}) copy-start(f32[1024,1024]{0,1:T(8,128)} %get-tuple-element.459) | copy-start | bytes 12582916 | tf_op jit(solution)/shard_map/while
  200.1 12.1 %copy-start.6 = (f32[1024,1024]{0,1:T(8,128)S(1)}, f32[1024,1024]{0,1:T(8,128)}, u32[]{:S(2)}) copy-start(f32[1024,1024]{0,1:T(8,128)} %get-tuple-element.459) | copy-start | bytes 12582916 | tf_op jit(solution)/shard_map/while
  229.2 12.1 %copy-start.6 = (f32[1024,1024]{0,1:T(8,128)S(1)}, f32[1024,1024]{0,1:T(8,128)}, u32[]{:S(2)}) copy-start(f32[1024,1024]{0,1:T(8,128)} %get-tuple-element.459) | copy-start | bytes 12582916 | tf_op jit(solution)/shard_map/while
  258.3 12.1 %copy-start.6 = (f32[1024,1024]{0,1:T(8,128)S(1)}, f32[1024,1024]{0,1:T(8,128)}, u32[]{:S(2)}) copy-start(f32[1024,1024]{0,1:T(8,128)} %get-tuple-element.459) | copy-start | bytes 12582916 | tf_op jit(solution)/shard_map/while
  287.5 12.1 %copy-start.6 = (f32[1024,1024]{0,1:T(8,128)S(1)}, f32[1024,1024]{0,1:T(8,128)}, u32[]{:S(2)}) copy-start(f32[1024,1024]{0,1:T(8,128)} %get-tuple-element.459) | copy-start | bytes 12582916 | tf_op jit(solution)/shard_map/while
  316.6 12.1 %copy-start.6 = (f32[1024,1024]{0,1:T(8,128)S(1)}, f32[1024,1024]{0,1:T(8,128)}, u32[]{:S(2)}) copy-start(f32[1024,1024]{0,1:T(8,128)} %get-tuple-element.459) | copy-start | bytes 12582916 | tf_op jit(solution)/shard_map/while
  345.7 12.1 %copy-start.6 = (f32[1024,1024]{0,1:T(8,128)S(1)}, f32[1024,1024]{0,1:T(8,128)}, u32[]{:S(2)}) copy-start(f32[1024,1024]{0,1:T(8,128)} %get-tuple-element.459) | copy-start | bytes 12582916 | tf_op jit(solution)/shard_map/while
  374.8 12.1 %copy-start.6 = (f32[1024,1024]{0,1:T(8,128)S(1)}, f32[1024,1024]{0,1:T(8,128)}, u32[]{:S(2)}) copy-start(f32[1024,1024]{0,1:T(8,128)} %get-tuple-element.459) | copy-start | bytes 12582916 | tf_op jit(solution)/shard_map/while
  403.9 12.1 %copy-start.6 = (f32[1024,1024]{0,1:T(8,128)S(1)}, f32[1024,1024]{0,1:T(8,128)}, u32[]{:S(2)}) copy-start(f32[1024,1024]{0,1:T(8,128)} %get-tuple-element.459) | copy-start | bytes 12582916 | tf_op jit(solution)/shard_map/while
  433.0 12.1 %copy-start.6 = (f32[1024,1024]{0,1:T(8,128)S(1)}, f32[1024,1024]{0,1:T(8,128)}, u32[]{:S(2)}) copy-start(f32[1024,1024]{0,1:T(8,128)} %get-tuple-element.459) | copy-start | bytes 12582916 | tf_op jit(solution)/shard_map/while
  462.1 12.1 %copy-start.6 = (f32[1024,1024]{0,1:T(8,128)S(1)}, f32[1024,1024]{0,1:T(8,128)}, u32[]{:S(2)}) copy-start(f32[1024,1024]{0,1:T(8,128)} %get-tuple-element.459) | copy-start | bytes 12582916 | tf_op jit(solution)/shard_map/while
  491.2 12.1 %copy-start.6 = (f32[1024,1024]{0,1:T(8,128)S(1)}, f32[1024,1024]{0,1:T(8,128)}, u32[]{:S(2)}) copy-start(f32[1024,1024]{0,1:T(8,128)} %get-tuple-element.459) | copy-start | bytes 12582916 | tf_op jit(solution)/shard_map/while
  520.3 12.1 %copy-start.6 = (f32[1024,1024]{0,1:T(8,128)S(1)}, f32[1024,1024]{0,1:T(8,128)}, u32[]{:S(2)}) copy-start(f32[1024,1024]{0,1:T(8,128)} %get-tuple-element.459) | copy-start | bytes 12582916 | tf_op jit(solution)/shard_map/while
  549.4 12.1 %copy-start.6 = (f32[1024,1024]{0,1:T(8,128)S(1)}, f32[1024,1024]{0,1:T(8,128)}, u32[]{:S(2)}) copy-start(f32[1024,1024]{0,1:T(8,128)} %get-tuple-element.459) | copy-start | bytes 12582916 | tf_op jit(solution)/shard_map/while
  578.5 12.1 %copy-start.6 = (f32[1024,1024]{0,1:T(8,128)S(1)}, f32[1024,1024]{0,1:T(8,128)}, u32[]{:S(2)}) copy-start(f32[1024,1024]{0,1:T(8,128)} %get-tuple-element.459) | copy-start | bytes 12582916 | tf_op jit(solution)/shard_map/while
  607.6 12.1 %copy-start.6 = (f32[1024,1024]{0,1:T(8,128)S(1)}, f32[1024,1024]{0,1:T(8,128)}, u32[]{:S(2)}) copy-start(f32[1024,1024]{0,1:T(8,128)} %get-tuple-element.459) | copy-start | bytes 12582916 | tf_op jit(solution)/shard_map/while
  636.8 26.9 %copy-start.3 = (f32[1024,1024]{0,1:T(8,128)S(1)}, f32[1024,1024]{0,1:T(8,128)}, u32[]{:S(2)}) copy-start(f32[1024,1024]{0,1:T(8,128)} %get-tuple-element.96) | copy-start | bytes 12582916
  661.2 24.5 %collective-permute-start.4 = (f32[1,16,128,64]{2,3,1,0:T(8,128)S(1)}, f32[1,16,128,64]{2,3,1,0:T(8,128)S(1)}, u32[]{:S(2)}, u32[]{:S(2)}) collective-permute-start(f32[1,16,128,64]{2,3,1,0:T(8,128)S(1)} %get-tuple-element.285), channel_id=1, source_target_pairs={{0,16},{4,20},{8,24},{12,28},{16,0},{20,4},{24,8},{28,12},{1,17},{... | collective-permute-start | bytes 1572872 | tf_op jit(solution)/shard_map/ppermute | solution.py:10
  671.4 51.1 %reduce-scatter.3.cloned.1.call-start = ((), (), s32[]{:S(2)}) async-start(), calls=%async_computation.2 | async-start | bytes 655360 | tf_op jit(solution)/shard_map/reduce_scatter | solution.py:158
  671.5 18.9 %copy-start.2 = (f32[16,1024,64]{1,2,0:T(8,128)S(1)}, f32[16,1024,64]{1,2,0:T(8,128)}, u32[]{:S(2)}) copy-start(f32[16,1024,64]{1,2,0:T(8,128)} %get-tuple-element.472) | copy-start | bytes 12582916
  685.8 11.3 %copy-start.4 = (f32[1024,1024]{0,1:T(8,128)S(1)}, f32[1024,1024]{0,1:T(8,128)}, u32[]{:S(2)}) copy-start(f32[1024,1024]{0,1:T(8,128)} %get-tuple-element.96) | copy-start | bytes 12582916
  (3 other events, 15.8 us)
Sparse Core Ops, SparseCore 0:
  20.0 76.3 all-gather.3
  671.5 19.2 reduce-scatter.4
  701.5 20.9 reduce-scatter.2
where the time goes:
time: 737 us; the launch traced here: 729 us
  matrix products  440 us (60%)
  other arithmetic  91.3 us (12%)
  local copies, waits for them, and re-layouts  75.5 us (10%)
  waiting for transfers between devices  73.7 us (10%)
  blocking collectives  21.2 us (3%)
  between operations  18.3 us (2%)
  starting transfers between devices  8.59 us (1%)
    dot_general x16, matrix products, head_step(): inner = jnp.dot(cot_one, x_one.T, precision=highest)  194 us
    dot_general x16, matrix products, head_step(): grad_x_one = jnp.dot(weighted.T, cot_one, precision=highest)  151 us
    reduce_sum x16, other arithmetic, head_step(): jnp.sum(jnp.where(local_level == level, plain, 0.0), axis=1)  66 us
    all_gather x1, waiting for transfers between devices, local(): lax.all_gather(tail_total[None], 'seq', axis=0, tiled=True)  33.9 us
    ppermute x5, waiting for transfers between devices, from_partner(): lax.ppermute(x, axis, [(i, i ^ 1 << apart) for i in range(lax.axis_size(a...  31.6 us
    dynamic_update_slice x32, local copies, waits for them, and re-layouts, local(): lax.scan(head_step, jnp.zeros((rows_dev, rows_dev), jnp.float32), pieces)  26.7 us
    dot_general x1, matrix products, local(): jnp.einsum('kthp,khnp->tn', weighted_cot, fwd_state, precision=highest)  22.2 us
    unnamed x1, blocking collectives  21.2 us
  transfers between devices with their start and end apart: 8, of which 5 were waited for; matrix products, arithmetic and copies ran while one was open for 76% of the time, Pallas kernels for 0%

commit v1 on v0

--- a/solution.py
+++ b/solution.py
@@ -4,6 +4,28 @@
 from jax.sharding import PartitionSpec as P
 
 STRETCH = 64
+
+
+def laid_out(blocks, dim):
+    blocks = jnp.moveaxis(blocks, 0, dim)
+    shape = blocks.shape
+    return blocks.reshape(*shape[:dim], shape[dim] * shape[dim + 1], *shape[dim + 2 :])
+
+
+def ring_gather(x, axis, dim):
+    peers = lax.axis_size(axis)
+    pairs = [(i, (i + 1) % peers) for i in range(peers)]
+    back = [(b, a) for a, b in pairs]
+    lower, upper = ([], [])
+    for step in range(peers - 1):
+        if step % 2 == 0:
+            lower.append(lax.ppermute(lower[-1] if lower else x, axis, pairs))
+        else:
+            upper.append(lax.ppermute(upper[-1] if upper else x, axis, back))
+    parts = jnp.stack([*lower[::-1], x, *upper])
+    shift = lax.axis_index(axis) - len(lower)
+    parts = parts[(jnp.arange(peers) - shift) % peers]
+    return laid_out(parts, dim)
 
 
 def from_partner(x, axis, apart):
@@ -75,7 +97,7 @@
         after_clean = (1.0 - upper_half) * far_clean * after_clean + upper_half * after_clean
         own_clean = own_clean * far_clean
     all_tail, all_clean = (
-        lax.all_gather(tail_total[None], "seq", axis=0, tiled=True),
+        ring_gather(tail_total[None], "seq", 0),
         lax.all_gather(device_clean[None], "seq", axis=0, tiled=True),
     )
     zero_count = jnp.cumsum(1.0 - all_clean)

time: 737 us -> 766 us (1.039)
  local copies, waits for them, and re-layouts: 75.5 us -> 89.1 us
  starting transfers between devices: 8.59 us -> 21.1 us
    ppermute x0 -> x7, waiting for transfers between devices: none -> 34.8 us  [the longest x4 31.3 us: ring_gather(): lower.append(lax.ppermute(lower[-1] if lower else x, axis, pairs))]
    all_gather x1 -> x0, waiting for transfers between devices: 33.9 us -> none  [local(): lax.all_gather(tail_total[None], 'seq', axis=0, tiled=True)]
    ppermute x0 -> x7, starting transfers between devices: none -> 18.2 us  [the longest x3 10 us: ring_gather(): upper.append(lax.ppermute(upper[-1] if upper else x, axis, back))]
    unnamed x28 -> x33, local copies, waits for them, and re-layouts: 18.1 us -> 25.9 us
  transfers between devices with their start and end apart: 8 -> 14, of which waited for: 5 -> 7; matrix products, arithmetic and copies ran while one was open for 76% -> 74% of each run, Pallas kernels for 0% -> 0%
where the time goes in v1:
time: 766 us; the launch traced here: 758 us
  matrix products  439 us (57%)
  other arithmetic  92.4 us (12%)
  local copies, waits for them, and re-layouts  89.1 us (12%)
  waiting for transfers between devices  74.8 us (10%)
  blocking collectives  22.4 us (3%)
  starting transfers between devices  21.1 us (3%)
  between operations  18.6 us (2%)
    dot_general x16, matrix products, head_step(): inner = jnp.dot(cot_one, x_one.T, precision=highest)  194 us
    dot_general x16, matrix products, head_step(): grad_x_one = jnp.dot(weighted.T, cot_one, precision=highest)  151 us
    reduce_sum x16, other arithmetic, head_step(): jnp.sum(jnp.where(local_level == level, plain, 0.0), axis=1)  66 us
    ppermute x5, waiting for transfers between devices, from_partner(): lax.ppermute(x, axis, [(i, i ^ 1 << apart) for i in range(lax.axis_size(a...  33.2 us
    ppermute x4, waiting for transfers between devices, ring_gather(): lower.append(lax.ppermute(lower[-1] if lower else x, axis, pairs))  31.3 us
    dynamic_update_slice x32, local copies, waits for them, and re-layouts, local(): lax.scan(head_step, jnp.zeros((rows_dev, rows_dev), jnp.float32), pieces)  26.7 us
    unnamed x33, local copies, waits for them, and re-layouts  25.9 us
    unnamed x1, blocking collectives  22.4 us
  transfers between devices with their start and end apart: 14, of which 7 were waited for; matrix products, arithmetic and copies ran while one was open for 74% of the time, Pallas kernels for 0%

profile of v1, /device:TPU:0, one launch (start us, length us, event | category | flops | bytes accessed | tf_op | source)
XLA Modules:
  0.0 758.1 jit_solution(6514457014831514184)
XLA Ops:
  25.0 19.3 %collective-permute-done.5 = f32[1,16,128,64]{2,3,1,0:T(8,128)S(1)} collective-permute-done((f32[1,16,128,64]{2,3,1,0:T(8,128)S(1)}, f32[1,16,128,64]{2,3,1,0:T(8,128)S(1)}, u32[]{:S(2)}, u32[]{:S(2)}) %collective-permute-start.5) | collective-permute-done | bytes 524320 | tf_op jit(solution)/shard_map/ppermute | solution.py:22
  49.9 22.4 %all-reduce = f32[8]{0:T(128)S(1)} all-reduce(f32[8]{0:T(128)S(1)} %bitcast_dynamic-update-slice_fusion.8), channel_id=2, replica_groups=mesh['seq'=8,'head'=4] {'seq'}, use_global_device_ids=true, to_apply=%add | all-reduce | flops 8 | bytes 64
  80.9 12.0 %collective-permute-done.7 = f32[1,16,128,64]{2,3,1,0:T(8,128)S(1)} collective-permute-done((f32[1,16,128,64]{2,3,1,0:T(8,128)S(1)}, f32[1,16,128,64]{2,3,1,0:T(8,128)S(1)}, u32[]{:S(2)}, u32[]{:S(2)}) %collective-permute-start.7) | collective-permute-done | bytes 524320 | tf_op jit(solution)/shard_map/ppermute | solution.py:22
  136.2 11.6 %fusion.30 = f32[3,1024,16]{1,2,0:T(8,128)S(1)} fusion(f32[1024,16,64]{0,2,1:T(8,128)S(1)} %bitcast.222, f32[3,16,128,64]{2,0,3,1:T(4,128)S(1)} %fusion.38, f32[1024,128]{1,0:T(8,128)S(1)} %copy-done.5), kind=kOutput, calls=%fused_computation.51 | convolution fusion | flops 4838080512 | bytes 6488064 | tf_op jit(solution)/shard_map/tn,khnp->kthp/dot_general | solution.py:123
  149.6 11.2 %fusion.50 = f32[3,16,128,64]{2,3,1,0:T(8,128)} fusion(f32[3,1024,16]{1,2,0:T(8,128)S(1)} %get-tuple-element.255, f32[1024,16,64]{0,2,1:T(8,128)S(1)} %bitcast.223, f32[1024,128]{1,0:T(8,128)S(1)} %copy-done.5), kind=kOutput, calls=%fused_computation.74 | convolution fusion | flops 4834983936 | bytes 6488064 | tf_op jit(solution)/shard_map/tn,kthp->khnp/dot_general | solution.py:69
  178.7 17.4 %collective-permute-done.2 = f32[3,16,128,64]{2,3,1,0:T(8,128)} collective-permute-done((f32[3,16,128,64]{2,3,1,0:T(8,128)}, f32[3,16,128,64]{2,3,1,0:T(8,128)}, u32[]{:S(2)}, u32[]{:S(2)}) %collective-permute-start.2) | collective-permute-done | bytes 1572896 | tf_op jit(solution)/shard_map/ppermute | solution.py:32
  200.2 465.9 %while.16 = (s32[]{:T(128)}, f32[1024,1024]{0,1:T(8,128)}, f32[16,1024,64]{1,2,0:T(8,128)}, f32[16,5,1024]{2,0,1:T(8,128)}, f32[16,1024]{1,0:T(8,128)}, /*index=...) while((s32[]{:T(128)}, f32[1024,1024]{0,1:T(8,128)}, ...), condition=%wide.region_7.8_spmd.clone.clone, body=%wide.region_1.7_spmd.clone.clone.sunk | while | flops 1703930880 | bytes 43289372 | solution.py:167
  202.1 11.7 %multiply_multiply_fusion.4 = (f32[1024,1024]{0,1:T(8,128)S(1)}, f32[1024,1024]{0,1:T(8,128)}) fusion(f32[1024,1024]{0,1:T(8,128)} %get-tuple-element.427, s32[1024]{0:T(1024)S(1)} %get-tuple-element.428, f32[1024]{0:T(1024)S(1)} %bitcast.240, f32[1024]{0:T(1024)S(1)} %bitcast.242, f32[1024]{0:T(1024)S(1)} %bitcast.252, f32[1024]{0:T(1024)S(1)} %bitcast.246, ...), kind=kOutput, calls=%fused_computation.15.clone.1 | convolution fusion | flops 839909376 | bytes 17348096 | tf_op jit(solution)/shard_map/while/body/eval_jaxpr/dot_general | solution.py:147
  230.7 12.1 %multiply_multiply_fusion.4 = (f32[1024,1024]{0,1:T(8,128)S(1)}, f32[1024,1024]{0,1:T(8,128)}) fusion(f32[1024,1024]{0,1:T(8,128)} %get-tuple-element.427, s32[1024]{0:T(1024)S(1)} %get-tuple-element.428, f32[1024]{0:T(1024)S(1)} %bitcast.240, f32[1024]{0:T(1024)S(1)} %bitcast.242, f32[1024]{0:T(1024)S(1)} %bitcast.252, f32[1024]{0:T(1024)S(1)} %bitcast.246, ...), kind=kOutput, calls=%fused_computation.15.clone.1 | convolution fusion | flops 839909376 | bytes 17348096 | tf_op jit(solution)/shard_map/while/body/eval_jaxpr/dot_general | solution.py:147
  259.8 12.1 %multiply_multiply_fusion.4 = (f32[1024,1024]{0,1:T(8,128)S(1)}, f32[1024,1024]{0,1:T(8,128)}) fusion(f32[1024,1024]{0,1:T(8,128)} %get-tuple-element.427, s32[1024]{0:T(1024)S(1)} %get-tuple-element.428, f32[1024]{0:T(1024)S(1)} %bitcast.240, f32[1024]{0:T(1024)S(1)} %bitcast.242, f32[1024]{0:T(1024)S(1)} %bitcast.252, f32[1024]{0:T(1024)S(1)} %bitcast.246, ...), kind=kOutput, calls=%fused_computation.15.clone.1 | convolution fusion | flops 839909376 | bytes 17348096 | tf_op jit(solution)/shard_map/while/body/eval_jaxpr/dot_general | solution.py:147
  272.0 9.5 %fusion.105 = f32[16,1024,64]{1,2,0:T(8,128)} fusion(f32[16,1024,64]{1,2,0:T(8,128)} %get-tuple-element.402, s32[]{:T(128)S(6)} %copy.84, f32[1024,1024]{0,1:T(8,128)S(1)} %copy-done.6, f32[1024]{0:T(1024)S(1)} %bitcast.253, f32[1024]{0:T(1024)S(1)} %bitcast.247, f32[1024]{0:T(1024)S(1)} %bitcast.249, f32[1024]{0:T(1024)S(1)} %bitcast.251, ...), kind=kOutput, calls=%fused_computation.27.clone.1 | convolution fusion | flops 835715072 | bytes 4764672 | tf_op jit(solution)/shard_map/while/body/eval_jaxpr/dot_general | solution.py:151
  289.0 12.1 %multiply_multiply_fusion.4 = (f32[1024,1024]{0,1:T(8,128)S(1)}, f32[1024,1024]{0,1:T(8,128)}) fusion(f32[1024,1024]{0,1:T(8,128)} %get-tuple-element.427, s32[1024]{0:T(1024)S(1)} %get-tuple-element.428, f32[1024]{0:T(1024)S(1)} %bitcast.240, f32[1024]{0:T(1024)S(1)} %bitcast.242, f32[1024]{0:T(1024)S(1)} %bitcast.252, f32[1024]{0:T(1024)S(1)} %bitcast.246, ...), kind=kOutput, calls=%fused_computation.15.clone.1 | convolution fusion | flops 839909376 | bytes 17348096 | tf_op jit(solution)/shard_map/while/body/eval_jaxpr/dot_general | solution.py:147
  301.1 9.5 %fusion.105 = f32[16,1024,64]{1,2,0:T(8,128)} fusion(f32[16,1024,64]{1,2,0:T(8,128)} %get-tuple-element.402, s32[]{:T(128)S(6)} %copy.84, f32[1024,1024]{0,1:T(8,128)S(1)} %copy-done.6, f32[1024]{0:T(1024)S(1)} %bitcast.253, f32[1024]{0:T(1024)S(1)} %bitcast.247, f32[1024]{0:T(1024)S(1)} %bitcast.249, f32[1024]{0:T(1024)S(1)} %bitcast.251, ...), kind=kOutput, calls=%fused_computation.27.clone.1 | convolution fusion | flops 835715072 | bytes 4764672 | tf_op jit(solution)/shard_map/while/body/eval_jaxpr/dot_general | solution.py:151
  318.1 12.1 %multiply_multiply_fusion.4 = (f32[1024,1024]{0,1:T(8,128)S(1)}, f32[1024,1024]{0,1:T(8,128)}) fusion(f32[1024,1024]{0,1:T(8,128)} %get-tuple-element.427, s32[1024]{0:T(1024)S(1)} %get-tuple-element.428, f32[1024]{0:T(1024)S(1)} %bitcast.240, f32[1024]{0:T(1024)S(1)} %bitcast.242, f32[1024]{0:T(1024)S(1)} %bitcast.252, f32[1024]{0:T(1024)S(1)} %bitcast.246, ...), kind=kOutput, calls=%fused_computation.15.clone.1 | convolution fusion | flops 839909376 | bytes 17348096 | tf_op jit(solution)/shard_map/while/body/eval_jaxpr/dot_general | solution.py:147
  347.2 12.1 %multiply_multiply_fusion.4 = (f32[1024,1024]{0,1:T(8,128)S(1)}, f32[1024,1024]{0,1:T(8,128)}) fusion(f32[1024,1024]{0,1:T(8,128)} %get-tuple-element.427, s32[1024]{0:T(1024)S(1)} %get-tuple-element.428, f32[1024]{0:T(1024)S(1)} %bitcast.240, f32[1024]{0:T(1024)S(1)} %bitcast.242, f32[1024]{0:T(1024)S(1)} %bitcast.252, f32[1024]{0:T(1024)S(1)} %bitcast.246, ...), kind=kOutput, calls=%fused_computation.15.clone.1 | convolution fusion | flops 839909376 | bytes 17348096 | tf_op jit(solution)/shard_map/while/body/eval_jaxpr/dot_general | solution.py:147
  359.3 9.5 %fusion.105 = f32[16,1024,64]{1,2,0:T(8,128)} fusion(f32[16,1024,64]{1,2,0:T(8,128)} %get-tuple-element.402, s32[]{:T(128)S(6)} %copy.84, f32[1024,1024]{0,1:T(8,128)S(1)} %copy-done.6, f32[1024]{0:T(1024)S(1)} %bitcast.253, f32[1024]{0:T(1024)S(1)} %bitcast.247, f32[1024]{0:T(1024)S(1)} %bitcast.249, f32[1024]{0:T(1024)S(1)} %bitcast.251, ...), kind=kOutput, calls=%fused_computation.27.clone.1 | convolution fusion | flops 835715072 | bytes 4764672 | tf_op jit(solution)/shard_map/while/body/eval_jaxpr/dot_general | solution.py:151
  376.3 12.1 %multiply_multiply_fusion.4 = (f32[1024,1024]{0,1:T(8,128)S(1)}, f32[1024,1024]{0,1:T(8,128)}) fusion(f32[1024,1024]{0,1:T(8,128)} %get-tuple-element.427, s32[1024]{0:T(1024)S(1)} %get-tuple-element.428, f32[1024]{0:T(1024)S(1)} %bitcast.240, f32[1024]{0:T(1024)S(1)} %bitcast.242, f32[1024]{0:T(1024)S(1)} %bitcast.252, f32[1024]{0:T(1024)S(1)} %bitcast.246, ...), kind=kOutput, calls=%fused_computation.15.clone.1 | convolution fusion | flops 839909376 | bytes 17348096 | tf_op jit(solution)/shard_map/while/body/eval_jaxpr/dot_general | solution.py:147
  388.5 9.5 %fusion.105 = f32[16,1024,64]{1,2,0:T(8,128)} fusion(f32[16,1024,64]{1,2,0:T(8,128)} %get-tuple-element.402, s32[]{:T(128)S(6)} %copy.84, f32[1024,1024]{0,1:T(8,128)S(1)} %copy-done.6, f32[1024]{0:T(1024)S(1)} %bitcast.253, f32[1024]{0:T(1024)S(1)} %bitcast.247, f32[1024]{0:T(1024)S(1)} %bitcast.249, f32[1024]{0:T(1024)S(1)} %bitcast.251, ...), kind=kOutput, calls=%fused_computation.27.clone.1 | convolution fusion | flops 835715072 | bytes 4764672 | tf_op jit(solution)/shard_map/while/body/eval_jaxpr/dot_general | solution.py:151
  405.4 12.1 %multiply_multiply_fusion.4 = (f32[1024,1024]{0,1:T(8,128)S(1)}, f32[1024,1024]{0,1:T(8,128)}) fusion(f32[1024,1024]{0,1:T(8,128)} %get-tuple-element.427, s32[1024]{0:T(1024)S(1)} %get-tuple-element.428, f32[1024]{0:T(1024)S(1)} %bitcast.240, f32[1024]{0:T(1024)S(1)} %bitcast.242, f32[1024]{0:T(1024)S(1)} %bitcast.252, f32[1024]{0:T(1024)S(1)} %bitcast.246, ...), kind=kOutput, calls=%fused_computation.15.clone.1 | convolution fusion | flops 839909376 | bytes 17348096 | tf_op jit(solution)/shard_map/while/body/eval_jaxpr/dot_general | solution.py:147
  434.5 12.1 %multiply_multiply_fusion.4 = (f32[1024,1024]{0,1:T(8,128)S(1)}, f32[1024,1024]{0,1:T(8,128)}) fusion(f32[1024,1024]{0,1:T(8,128)} %get-tuple-element.427, s32[1024]{0:T(1024)S(1)} %get-tuple-element.428, f32[1024]{0:T(1024)S(1)} %bitcast.240, f32[1024]{0:T(1024)S(1)} %bitcast.242, f32[1024]{0:T(1024)S(1)} %bitcast.252, f32[1024]{0:T(1024)S(1)} %bitcast.246, ...), kind=kOutput, calls=%fused_computation.15.clone.1 | convolution fusion | flops 839909376 | bytes 17348096 | tf_op jit(solution)/shard_map/while/body/eval_jaxpr/dot_general | solution.py:147
  446.7 9.5 %fusion.105 = f32[16,1024,64]{1,2,0:T(8,128)} fusion(f32[16,1024,64]{1,2,0:T(8,128)} %get-tuple-element.402, s32[]{:T(128)S(6)} %copy.84, f32[1024,1024]{0,1:T(8,128)S(1)} %copy-done.6, f32[1024]{0:T(1024)S(1)} %bitcast.253, f32[1024]{0:T(1024)S(1)} %bitcast.247, f32[1024]{0:T(1024)S(1)} %bitcast.249, f32[1024]{0:T(1024)S(1)} %bitcast.251, ...), kind=kOutput, calls=%fused_computation.27.clone.1 | convolution fusion | flops 835715072 | bytes 4764672 | tf_op jit(solution)/shard_map/while/body/eval_jaxpr/dot_general | solution.py:151
  463.7 12.1 %multiply_multiply_fusion.4 = (f32[1024,1024]{0,1:T(8,128)S(1)}, f32[1024,1024]{0,1:T(8,128)}) fusion(f32[1024,1024]{0,1:T(8,128)} %get-tuple-element.427, s32[1024]{0:T(1024)S(1)} %get-tuple-element.428, f32[1024]{0:T(1024)S(1)} %bitcast.240, f32[1024]{0:T(1024)S(1)} %bitcast.242, f32[1024]{0:T(1024)S(1)} %bitcast.252, f32[1024]{0:T(1024)S(1)} %bitcast.246, ...), kind=kOutput, calls=%fused_computation.15.clone.1 | convolution fusion | flops 839909376 | bytes 17348096 | tf_op jit(solution)/shard_map/while/body/eval_jaxpr/dot_general | solution.py:147
  475.8 9.5 %fusion.105 = f32[16,1024,64]{1,2,0:T(8,128)} fusion(f32[16,1024,64]{1,2,0:T(8,128)} %get-tuple-element.402, s32[]{:T(128)S(6)} %copy.84, f32[1024,1024]{0,1:T(8,128)S(1)} %copy-done.6, f32[1024]{0:T(1024)S(1)} %bitcast.253, f32[1024]{0:T(1024)S(1)} %bitcast.247, f32[1024]{0:T(1024)S(1)} %bitcast.249, f32[1024]{0:T(1024)S(1)} %bitcast.251, ...), kind=kOutput, calls=%fused_computation.27.clone.1 | convolution fusion | flops 835715072 | bytes 4764672 | tf_op jit(solution)/shard_map/while/body/eval_jaxpr/dot_general | solution.py:151
  492.8 12.1 %multiply_multiply_fusion.4 = (f32[1024,1024]{0,1:T(8,128)S(1)}, f32[1024,1024]{0,1:T(8,128)}) fusion(f32[1024,1024]{0,1:T(8,128)} %get-tuple-element.427, s32[1024]{0:T(1024)S(1)} %get-tuple-element.428, f32[1024]{0:T(1024)S(1)} %bitcast.240, f32[1024]{0:T(1024)S(1)} %bitcast.242, f32[1024]{0:T(1024)S(1)} %bitcast.252, f32[1024]{0:T(1024)S(1)} %bitcast.246, ...), kind=kOutput, calls=%fused_computation.15.clone.1 | convolution fusion | flops 839909376 | bytes 17348096 | tf_op jit(solution)/shard_map/while/body/eval_jaxpr/dot_general | solution.py:147
  521.9 12.1 %multiply_multiply_fusion.4 = (f32[1024,1024]{0,1:T(8,128)S(1)}, f32[1024,1024]{0,1:T(8,128)}) fusion(f32[1024,1024]{0,1:T(8,128)} %get-tuple-element.427, s32[1024]{0:T(1024)S(1)} %get-tuple-element.428, f32[1024]{0:T(1024)S(1)} %bitcast.240, f32[1024]{0:T(1024)S(1)} %bitcast.242, f32[1024]{0:T(1024)S(1)} %bitcast.252, f32[1024]{0:T(1024)S(1)} %bitcast.246, ...), kind=kOutput, calls=%fused_computation.15.clone.1 | convolution fusion | flops 839909376 | bytes 17348096 | tf_op jit(solution)/shard_map/while/body/eval_jaxpr/dot_general | solution.py:147
  551.0 12.1 %multiply_multiply_fusion.4 = (f32[1024,1024]{0,1:T(8,128)S(1)}, f32[1024,1024]{0,1:T(8,128)}) fusion(f32[1024,1024]{0,1:T(8,128)} %get-tuple-element.427, s32[1024]{0:T(1024)S(1)} %get-tuple-element.428, f32[1024]{0:T(1024)S(1)} %bitcast.240, f32[1024]{0:T(1024)S(1)} %bitcast.242, f32[1024]{0:T(1024)S(1)} %bitcast.252, f32[1024]{0:T(1024)S(1)} %bitcast.246, ...), kind=kOutput, calls=%fused_computation.15.clone.1 | convolution fusion | flops 839909376 | bytes 17348096 | tf_op jit(solution)/shard_map/while/body/eval_jaxpr/dot_general | solution.py:147
  580.1 12.1 %multiply_multiply_fusion.4 = (f32[1024,1024]{0,1:T(8,128)S(1)}, f32[1024,1024]{0,1:T(8,128)}) fusion(f32[1024,1024]{0,1:T(8,128)} %get-tuple-element.427, s32[1024]{0:T(1024)S(1)} %get-tuple-element.428, f32[1024]{0:T(1024)S(1)} %bitcast.240, f32[1024]{0:T(1024)S(1)} %bitcast.242, f32[1024]{0:T(1024)S(1)} %bitcast.252, f32[1024]{0:T(1024)S(1)} %bitcast.246, ...), kind=kOutput, calls=%fused_computation.15.clone.1 | convolution fusion | flops 839909376 | bytes 17348096 | tf_op jit(solution)/shard_map/while/body/eval_jaxpr/dot_general | solution.py:147
  609.1 12.1 %multiply_multiply_fusion.4 = (f32[1024,1024]{0,1:T(8,128)S(1)}, f32[1024,1024]{0,1:T(8,128)}) fusion(f32[1024,1024]{0,1:T(8,128)} %get-tuple-element.427, s32[1024]{0:T(1024)S(1)} %get-tuple-element.428, f32[1024]{0:T(1024)S(1)} %bitcast.240, f32[1024]{0:T(1024)S(1)} %bitcast.242, f32[1024]{0:T(1024)S(1)} %bitcast.252, f32[1024]{0:T(1024)S(1)} %bitcast.246, ...), kind=kOutput, calls=%fused_computation.15.clone.1 | convolution fusion | flops 839909376 | bytes 17348096 | tf_op jit(solution)/shard_map/while/body/eval_jaxpr/dot_general | solution.py:147
  638.2 12.1 %multiply_multiply_fusion.4 = (f32[1024,1024]{0,1:T(8,128)S(1)}, f32[1024,1024]{0,1:T(8,128)}) fusion(f32[1024,1024]{0,1:T(8,128)} %get-tuple-element.427, s32[1024]{0:T(1024)S(1)} %get-tuple-element.428, f32[1024]{0:T(1024)S(1)} %bitcast.240, f32[1024]{0:T(1024)S(1)} %bitcast.242, f32[1024]{0:T(1024)S(1)} %bitcast.252, f32[1024]{0:T(1024)S(1)} %bitcast.246, ...), kind=kOutput, calls=%fused_computation.15.clone.1 | convolution fusion | flops 839909376 | bytes 17348096 | tf_op jit(solution)/shard_map/while/body/eval_jaxpr/dot_general | solution.py:147
  650.4 9.5 %fusion.105 = f32[16,1024,64]{1,2,0:T(8,128)} fusion(f32[16,1024,64]{1,2,0:T(8,128)} %get-tuple-element.402, s32[]{:T(128)S(6)} %copy.84, f32[1024,1024]{0,1:T(8,128)S(1)} %copy-done.6, f32[1024]{0:T(1024)S(1)} %bitcast.253, f32[1024]{0:T(1024)S(1)} %bitcast.247, f32[1024]{0:T(1024)S(1)} %bitcast.249, f32[1024]{0:T(1024)S(1)} %bitcast.251, ...), kind=kOutput, calls=%fused_computation.27.clone.1 | convolution fusion | flops 835715072 | bytes 4764672 | tf_op jit(solution)/shard_map/while/body/eval_jaxpr/dot_general | solution.py:151
  667.4 22.2 %fusion.53 = f32[1024,128]{1,0:T(8,128)S(1)} fusion(f32[3,16,128,64]{2,0,3,1:T(4,128)S(1)} %fusion.38, f32[3,1024,16]{1,2,0:T(8,128)} %get-tuple-element.254, f32[1024,16,64]{0,2,1:T(8,128)} %bitcast.224), kind=kOutput, calls=%fused_computation.75 | convolution fusion | flops 4834983936 | bytes 6488064 | tf_op jit(solution)/shard_map/kthp,khnp->tn/dot_general | solution.py:122
  701.3 14.3 %collective-permute-done.4 = f32[1,16,128,64]{2,3,1,0:T(8,128)S(1)} collective-permute-done((f32[1,16,128,64]{2,3,1,0:T(8,128)S(1)}, f32[1,16,128,64]{2,3,1,0:T(8,128)S(1)}, u32[]{:S(2)}, u32[]{:S(2)}) %collective-permute-start.4) | collective-permute-done | bytes 524320 | tf_op jit(solution)/shard_map/ppermute | solution.py:32
  (261 shorter events, 347.9 us)
Async XLA Ops:
  7.2 737.1 %reduce-scatter.5.cloned.1.call-start = ((), (), s32[]{:S(2)}) async-start(), calls=%async_computation.3 | async-start | bytes 655360 | tf_op jit(solution)/shard_map/reduce_scatter | solution.py:181
  12.7 34.8 %copy-start.10 = (u32[32]{0:T(128)S(1)}, u32[32]{0:T(128)}, u32[]{:S(2)}) copy-start(u32[32]{0:T(128)} %constant.194) | copy-start | bytes 388
  18.9 25.4 %collective-permute-start.5 = (f32[1,16,128,64]{2,3,1,0:T(8,128)S(1)}, f32[1,16,128,64]{2,3,1,0:T(8,128)S(1)}, u32[]{:S(2)}, u32[]{:S(2)}) collective-permute-start(f32[1,16,128,64]{2,3,1,0:T(8,128)S(1)} %bitcast.232), channel_id=1, source_target_pairs={{0,4},{4,8},{8,12},{12,16},{16,20},{20,24},{24,28},{28,0},{1,5},{5... | collective-permute-start | bytes 1572872 | tf_op jit(solution)/shard_map/ppermute | solution.py:22
  21.9 54.6 %collective-permute-start.9 = (f32[1,16,128,64]{2,3,1,0:T(8,128)S(1)}, f32[1,16,128,64]{2,3,1,0:T(8,128)S(1)}, u32[]{:S(2)}, u32[]{:S(2)}) collective-permute-start(f32[1,16,128,64]{2,3,1,0:T(8,128)S(1)} %bitcast.233), channel_id=1, source_target_pairs={{4,0},{8,4},{12,8},{16,12},{20,16},{24,20},{28,24},{0,28},{5,1},{9... | collective-permute-start | bytes 1572872 | tf_op jit(solution)/shard_map/ppermute | solution.py:24
  44.3 29.2 %collective-permute-start.6 = (f32[1,16,128,64]{2,3,1,0:T(8,128)S(1)}, f32[1,16,128,64]{2,3,1,0:T(8,128)S(1)}, u32[]{:S(2)}, u32[]{:S(2)}) collective-permute-start(f32[1,16,128,64]{2,3,1,0:T(8,128)S(1)} %collective-permute-done.5), channel_id=1, source_target_pairs={{0,4},{4,8},{8,12},{12,16},{16,20},{20,24},{24,28},{28,0},{1,5},{5... | collective-permute-start | bytes 1572872 | tf_op jit(solution)/shard_map/ppermute | solution.py:22
  49.3 53.4 %collective-permute-start = (f32[]{:T(128)}, f32[]{:T(128)}, u32[]{:S(2)}, u32[]{:S(2)}) collective-permute-start(f32[]{:T(128)} %bitcast.26), channel_id=1, source_target_pairs={{0,4},{4,0},{8,12},{12,8},{16,20},{20,16},{24,28},{28,24},{1,5},{5... | collective-permute-start | bytes 20 | tf_op jit(solution)/shard_map/ppermute | solution.py:32
  73.5 19.5 %collective-permute-start.7 = (f32[1,16,128,64]{2,3,1,0:T(8,128)S(1)}, f32[1,16,128,64]{2,3,1,0:T(8,128)S(1)}, u32[]{:S(2)}, u32[]{:S(2)}) collective-permute-start(f32[1,16,128,64]{2,3,1,0:T(8,128)S(1)} %collective-permute-done.6), channel_id=1, source_target_pairs={{0,4},{4,8},{8,12},{12,16},{16,20},{20,24},{24,28},{28,0},{1,5},{5... | collective-permute-start | bytes 1572872 | tf_op jit(solution)/shard_map/ppermute | solution.py:22
  76.4 31.9 %collective-permute-start.10 = (f32[1,16,128,64]{2,3,1,0:T(8,128)S(1)}, f32[1,16,128,64]{2,3,1,0:T(8,128)}, u32[]{:S(2)}, u32[]{:S(2)}) collective-permute-start(f32[1,16,128,64]{2,3,1,0:T(8,128)S(1)} %collective-permute-done.9), channel_id=1, source_target_pairs={{4,0},{8,4},{12,8},{16,12},{20,16},{24,20},{28,24},{0,28},{5,1},{9... | collective-permute-start | bytes 1572872 | tf_op jit(solution)/shard_map/ppermute | solution.py:24
  92.9 17.8 %collective-permute-start.8 = (f32[1,16,128,64]{2,3,1,0:T(8,128)S(1)}, f32[1,16,128,64]{2,3,1,0:T(8,128)}, u32[]{:S(2)}, u32[]{:S(2)}) collective-permute-start(f32[1,16,128,64]{2,3,1,0:T(8,128)S(1)} %collective-permute-done.7), channel_id=1, source_target_pairs={{0,4},{4,8},{8,12},{12,16},{16,20},{20,24},{24,28},{28,0},{1,5},{5... | collective-permute-start | bytes 1572872 | tf_op jit(solution)/shard_map/ppermute | solution.py:22
  104.0 3.6 collective-permute-start.1
  108.3 13.8 %collective-permute-start.11 = (f32[1,16,128,64]{2,3,1,0:T(8,128)}, f32[1,16,128,64]{2,3,1,0:T(8,128)S(1)}, u32[]{:S(2)}, u32[]{:S(2)}) collective-permute-start(f32[1,16,128,64]{2,3,1,0:T(8,128)} %collective-permute-done.10), channel_id=1, source_target_pairs={{4,0},{8,4},{12,8},{16,12},{20,16},{24,20},{28,24},{0,28},{5,1},{9... | collective-permute-start | bytes 1572872 | tf_op jit(solution)/shard_map/ppermute | solution.py:24
  160.8 35.3 %collective-permute-start.2 = (f32[3,16,128,64]{2,3,1,0:T(8,128)}, f32[3,16,128,64]{2,3,1,0:T(8,128)}, u32[]{:S(2)}, u32[]{:S(2)}) collective-permute-start(f32[3,16,128,64]{2,3,1,0:T(8,128)} %fusion.50), channel_id=1, source_target_pairs={{0,4},{4,0},{8,12},{12,8},{16,20},{20,16},{24,28},{28,24},{1,5},{5... | collective-permute-start | bytes 4718600 | tf_op jit(solution)/shard_map/ppermute | solution.py:32
  200.2 489.4 %collective-permute-start.3 = (f32[2,16,128,64]{2,3,1,0:T(8,128)}, f32[2,16,128,64]{2,3,1,0:T(8,128)}, u32[]{:S(2)}, u32[]{:S(2)}) collective-permute-start(f32[2,16,128,64]{2,3,1,0:T(8,128)} %multiply_add_fusion), channel_id=1, source_target_pairs={{0,8},{4,12},{8,0},{12,4},{16,24},{20,28},{24,16},{28,20},{1,9},{5... | collective-permute-start | bytes 3145736 | tf_op jit(solution)/shard_map/ppermute | solution.py:32
  230.7 12.1 %copy-start.6 = (f32[1024,1024]{0,1:T(8,128)S(1)}, f32[1024,1024]{0,1:T(8,128)}, u32[]{:S(2)}) copy-start(f32[1024,1024]{0,1:T(8,128)} %get-tuple-element.427) | copy-start | bytes 12582916 | tf_op jit(solution)/shard_map/while
  259.8 12.1 %copy-start.6 = (f32[1024,1024]{0,1:T(8,128)S(1)}, f32[1024,1024]{0,1:T(8,128)}, u32[]{:S(2)}) copy-start(f32[1024,1024]{0,1:T(8,128)} %get-tuple-element.427) | copy-start | bytes 12582916 | tf_op jit(solution)/shard_map/while
  289.0 12.1 %copy-start.6 = (f32[1024,1024]{0,1:T(8,128)S(1)}, f32[1024,1024]{0,1:T(8,128)}, u32[]{:S(2)}) copy-start(f32[1024,1024]{0,1:T(8,128)} %get-tuple-element.427) | copy-start | bytes 12582916 | tf_op jit(solution)/shard_map/while
  318.1 12.1 %copy-start.6 = (f32[1024,1024]{0,1:T(8,128)S(1)}, f32[1024,1024]{0,1:T(8,128)}, u32[]{:S(2)}) copy-start(f32[1024,1024]{0,1:T(8,128)} %get-tuple-element.427) | copy-start | bytes 12582916 | tf_op jit(solution)/shard_map/while
  347.2 12.1 %copy-start.6 = (f32[1024,1024]{0,1:T(8,128)S(1)}, f32[1024,1024]{0,1:T(8,128)}, u32[]{:S(2)}) copy-start(f32[1024,1024]{0,1:T(8,128)} %get-tuple-element.427) | copy-start | bytes 12582916 | tf_op jit(solution)/shard_map/while
  376.3 12.1 %copy-start.6 = (f32[1024,1024]{0,1:T(8,128)S(1)}, f32[1024,1024]{0,1:T(8,128)}, u32[]{:S(2)}) copy-start(f32[1024,1024]{0,1:T(8,128)} %get-tuple-element.427) | copy-start | bytes 12582916 | tf_op jit(solution)/shard_map/while
  405.4 12.1 %copy-start.6 = (f32[1024,1024]{0,1:T(8,128)S(1)}, f32[1024,1024]{0,1:T(8,128)}, u32[]{:S(2)}) copy-start(f32[1024,1024]{0,1:T(8,128)} %get-tuple-element.427) | copy-start | bytes 12582916 | tf_op jit(solution)/shard_map/while
  434.5 12.1 %copy-start.6 = (f32[1024,1024]{0,1:T(8,128)S(1)}, f32[1024,1024]{0,1:T(8,128)}, u32[]{:S(2)}) copy-start(f32[1024,1024]{0,1:T(8,128)} %get-tuple-element.427) | copy-start | bytes 12582916 | tf_op jit(solution)/shard_map/while
  463.6 12.1 %copy-start.6 = (f32[1024,1024]{0,1:T(8,128)S(1)}, f32[1024,1024]{0,1:T(8,128)}, u32[]{:S(2)}) copy-start(f32[1024,1024]{0,1:T(8,128)} %get-tuple-element.427) | copy-start | bytes 12582916 | tf_op jit(solution)/shard_map/while
  492.8 12.1 %copy-start.6 = (f32[1024,1024]{0,1:T(8,128)S(1)}, f32[1024,1024]{0,1:T(8,128)}, u32[]{:S(2)}) copy-start(f32[1024,1024]{0,1:T(8,128)} %get-tuple-element.427) | copy-start | bytes 12582916 | tf_op jit(solution)/shard_map/while
  521.9 12.1 %copy-start.6 = (f32[1024,1024]{0,1:T(8,128)S(1)}, f32[1024,1024]{0,1:T(8,128)}, u32[]{:S(2)}) copy-start(f32[1024,1024]{0,1:T(8,128)} %get-tuple-element.427) | copy-start | bytes 12582916 | tf_op jit(solution)/shard_map/while
  551.0 12.1 %copy-start.6 = (f32[1024,1024]{0,1:T(8,128)S(1)}, f32[1024,1024]{0,1:T(8,128)}, u32[]{:S(2)}) copy-start(f32[1024,1024]{0,1:T(8,128)} %get-tuple-element.427) | copy-start | bytes 12582916 | tf_op jit(solution)/shard_map/while
  580.1 12.1 %copy-start.6 = (f32[1024,1024]{0,1:T(8,128)S(1)}, f32[1024,1024]{0,1:T(8,128)}, u32[]{:S(2)}) copy-start(f32[1024,1024]{0,1:T(8,128)} %get-tuple-element.427) | copy-start | bytes 12582916 | tf_op jit(solution)/shard_map/while
  609.1 12.1 %copy-start.6 = (f32[1024,1024]{0,1:T(8,128)S(1)}, f32[1024,1024]{0,1:T(8,128)}, u32[]{:S(2)}) copy-start(f32[1024,1024]{0,1:T(8,128)} %get-tuple-element.427) | copy-start | bytes 12582916 | tf_op jit(solution)/shard_map/while
  638.2 12.1 %copy-start.6 = (f32[1024,1024]{0,1:T(8,128)S(1)}, f32[1024,1024]{0,1:T(8,128)}, u32[]{:S(2)}) copy-start(f32[1024,1024]{0,1:T(8,128)} %get-tuple-element.427) | copy-start | bytes 12582916 | tf_op jit(solution)/shard_map/while
  667.4 24.9 %copy-start.3 = (f32[1024,1024]{0,1:T(8,128)S(1)}, f32[1024,1024]{0,1:T(8,128)}, u32[]{:S(2)}) copy-start(f32[1024,1024]{0,1:T(8,128)} %get-tuple-element.96) | copy-start | bytes 12582916
  691.8 23.8 %collective-permute-start.4 = (f32[1,16,128,64]{2,3,1,0:T(8,128)S(1)}, f32[1,16,128,64]{2,3,1,0:T(8,128)S(1)}, u32[]{:S(2)}, u32[]{:S(2)}) collective-permute-start(f32[1,16,128,64]{2,3,1,0:T(8,128)S(1)} %get-tuple-element.253), channel_id=1, source_target_pairs={{0,16},{4,20},{8,24},{12,28},{16,0},{20,4},{24,8},{28,12},{1,17},{... | collective-permute-start | bytes 1572872 | tf_op jit(solution)/shard_map/ppermute | solution.py:32
  700.0 51.1 %reduce-scatter.3.cloned.1.call-start = ((), (), s32[]{:S(2)}) async-start(), calls=%async_computation.2 | async-start | bytes 655360 | tf_op jit(solution)/shard_map/reduce_scatter | solution.py:180
  700.0 20.3 %copy-start.2 = (f32[16,1024,64]{1,2,0:T(8,128)S(1)}, f32[16,1024,64]{1,2,0:T(8,128)}, u32[]{:S(2)}) copy-start(f32[16,1024,64]{1,2,0:T(8,128)} %get-tuple-element.439) | copy-start | bytes 12582916
  (8 other events, 61.6 us)
Sparse Core Ops, SparseCore 0:
  700.1 22.3 reduce-scatter.4
  731.5 19.5 reduce-scatter.2
